TPU v7x, 32 devices: a whole 2x2x4 slice. The times are simulated.
32 devices in a mesh: shot: 2 (over y), col: 16 (over z, x, core).
Axes of the slice: x: 2, y: 2, z: 4, core: 2. Of those that a mesh axis runs over, the one named last changes fastest.
Arguments:
- wave_prev: float32 [256, 64, 512], P(('shot', 'col')), parts along dimension 0, may hold values from -6 to 6
- wave_now: float32 [256, 64, 512], P(('shot', 'col')), parts along dimension 0, may hold values from -6 to 6
- velocity: float32 [256, 64, 512], P(('shot', 'col')), parts along dimension 0, may hold values from 0.03 to 0.2
- source: bfloat16 [2, 256, 64, 512], P(None, ('shot', 'col')), parts along dimension 1, may hold values from -6 to 6
- active: int32 [2, 2048], P(None, ('shot', 'col')), parts along dimension 1, may hold values 0 or 1
- plan: int32 [2048], P(('shot', 'col')), parts along dimension 0, may hold values from 0 to 1023, as said below
- image_in: float32 [2048, 8, 4, 128], P(('shot', 'col')), parts along dimension 0, may hold values from -6 to 6
Outputs:
- wave_first: float32 [256, 64, 512], P(('shot', 'col')), parts along dimension 0
- wave_second: float32 [256, 64, 512], P(('shot', 'col')), parts along dimension 0
- image_out: float32 [2048, 8, 4, 128], P(('shot', 'col')), parts along dimension 0
There are 2 independent parts, one for each index of `shot`. A program takes and returns all parts, laid end to end along the dimension named above; each array names one. Nothing has to cross between parts.
Inputs may be any that keep to these rules, and one draw needn't show every extreme that they name: plan is a permutation of the 1024 brick numbers; the bricks of one device stand in at most 4 slot of any one device, and some pair of devices reaches 4.
All inputs are finite; a program needn't handle non-finite values. No bound on the sum of `active` on one device may be relied on, other than what follows from the above.
Results may differ from a plain program's by a relative error of at most 0.0003.
Values sent between devices are 32-bit elements; how exact they have to be, the bound alone decides.
A program may use at most 64 MiB of HBM per device.

v0:
```python
import jax
import jax.numpy as jnp
from jax import lax
from jax.sharding import PartitionSpec as P

NY = 64
NZ = 512
BY = 4
BZ = 128


STENCIL_COEF = (-205.0 / 72.0, 8.0 / 5.0, -1.0 / 5.0, 8.0 / 315.0, -1.0 / 560.0)


def with_halo(block, sides, width):
    for axis, dim in sides:
        count = lax.axis_size(axis)
        forward = [(i, i + 1) for i in range(count - 1)]
        backward = [(target, source) for source, target in forward]
        low = lax.ppermute(
            lax.slice_in_dim(block, block.shape[dim] - width, None, axis=dim), axis, forward
        )
        high = lax.ppermute(lax.slice_in_dim(block, 0, width, axis=dim), axis, backward)
        block = jnp.concatenate([low, block, high], axis=dim)
    return block


def laplace(widened):
    inner_rows = widened.shape[0] - 8
    breadth = widened.shape[1]
    length = widened.shape[2]
    centre = widened[4 : 4 + inner_rows]
    framed = jnp.pad(centre, ((0, 0), (4, 4), (4, 4)))
    summed = 3.0 * STENCIL_COEF[0] * centre
    for radius in range(1, 5):
        summed = summed + STENCIL_COEF[radius] * (
            widened[4 + radius : 4 + radius + inner_rows]
            + widened[4 - radius : 4 - radius + inner_rows]
            + framed[:, 4 + radius : 4 + radius + breadth, 4 : 4 + length]
            + framed[:, 4 - radius : 4 - radius + breadth, 4 : 4 + length]
            + framed[:, 4 : 4 + breadth, 4 + radius : 4 + radius + length]
            + framed[:, 4 : 4 + breadth, 4 - radius : 4 - radius + length]
        )
    return summed


def brick_mask(flags):
    grid = flags.astype(jnp.float32).reshape(NY // BY, NZ // BZ)
    return jnp.repeat(jnp.repeat(grid, BY, axis=0), BZ, axis=1)[None]


def shards(wave_prev, wave_now, velocity, source, active, plan, image_in):
    cells_x = wave_now.shape[0]
    mask_first = brick_mask(active[0])
    mask_second = brick_mask(active[1])
    previous = wave_prev
    current = wave_now
    results = []
    for masking in (mask_first, mask_second):
        widened = with_halo(current, (("col", 0),), 4)
        following = masking * (2.0 * current - previous + velocity * laplace(widened))
        results.append(following)
        previous = current
        current = following
    wave_first = results[0]
    wave_second = results[1]
    increment = (
        source[0].astype(jnp.float32) * wave_first + source[1].astype(jnp.float32) * wave_second
    )
    bricks = increment.reshape(cells_x, NY // BY, BY, NZ // BZ, BZ)
    bricks = bricks.transpose(1, 3, 0, 2, 4).reshape(-1, cells_x, BY, BZ)
    per_device = plan.shape[0]
    devices = lax.axis_size("col")
    myself = lax.axis_index("col")
    capacity = (per_device + devices - 1) // devices
    whole_plan = lax.all_gather(plan, "col", axis=0, tiled=True)
    owned = myself * per_device + jnp.arange(per_device, dtype=jnp.int32)
    slot_of = jnp.argmax(whole_plan[None, :] == owned[:, None], axis=1)
    target = slot_of // per_device
    slot_pos = slot_of % per_device
    send_rank = jnp.sum(
        (target[None, :] == target[:, None]) & (slot_pos[None, :] < slot_pos[:, None]), axis=1
    )
    outgoing = jnp.zeros((devices * capacity, cells_x, BY, BZ), jnp.float32)
    outgoing = outgoing.at[target * capacity + send_rank].set(bricks)
    incoming = lax.all_to_all(outgoing, "col", split_axis=0, concat_axis=0, tiled=True)
    anchor = plan // per_device
    order = jnp.arange(per_device, dtype=jnp.int32)
    recv_rank = jnp.sum(
        (anchor[None, :] == anchor[:, None]) & (order[None, :] < order[:, None]), axis=1
    )
    image_out = image_in + incoming[anchor * capacity + recv_rank]
    return (wave_first, wave_second, image_out)


def solution(mesh):
    in_specs = (
        P(("shot", "col"), None, None),
        P(("shot", "col"), None, None),
        P(("shot", "col"), None, None),
        P(None, ("shot", "col"), None, None),
        P(None, ("shot", "col")),
        P(("shot", "col")),
        P(("shot", "col"), None, None, None),
    )
    out_specs = (
        P(("shot", "col"), None, None),
        P(("shot", "col"), None, None),
        P(("shot", "col"), None, None, None),
    )
    return jax.shard_map(shards, mesh=mesh, in_specs=in_specs, out_specs=out_specs, check_vma=False)
```

profile of v0, /device:TPU:1, one launch (start us, length us, event | category | flops | bytes accessed | tf_op | source)
XLA Modules:
  0.0 93.0 jit_solution(14370527216062216220)
XLA Ops:
  0.6 0.0 copy-start.8
  0.6 0.0 copy-start
  0.7 0.0 copy-start.6
  0.7 0.0 copy-start.7
  0.7 2.3 %fusion.68 = (f32[4,64,512]{2,1,0:T(8,128)}, f32[4,64,512]{2,1,0:T(8,128)}) fusion(f32[8,64,512]{2,1,0:T(8,128)} %param.8), kind=kLoop, calls=%fused_computation.147 | loop fusion | bytes 2097152 | tf_op jit(solution)/shard_map/slice | solution.py:23
  3.0 4.5 %collective-permute-start.1 = (f32[4,64,512]{2,1,0:T(8,128)}, f32[4,64,512]{2,1,0:T(8,128)S(1)}, u32[]{:S(2)}, u32[]{:S(2)}) collective-permute-start(f32[4,64,512]{2,1,0:T(8,128)} %get-tuple-element.21), channel_id=1, source_target_pairs={{0,1},{1,2},{2,3},{3,4},{4,5},{5,6},{6,7},{7,8},{8,9},{9,10},{10,1... | collective-permute-start | bytes 1572872 | tf_op jit(solution)/shard_map/ppermute | solution.py:20
  7.5 1.9 %collective-permute-start = (f32[4,64,512]{2,1,0:T(8,128)}, f32[4,64,512]{2,1,0:T(8,128)S(1)}, u32[]{:S(2)}, u32[]{:S(2)}) collective-permute-start(f32[4,64,512]{2,1,0:T(8,128)} %get-tuple-element.20), channel_id=1, source_target_pairs={{1,0},{2,1},{3,2},{4,3},{5,4},{6,5},{7,6},{8,7},{9,8},{10,9},{11,1... | collective-permute-start | bytes 1572872 | tf_op jit(solution)/shard_map/ppermute | solution.py:23
  9.4 0.0 copy-done.6
  9.5 0.1 convert_element_type.36
  9.6 0.1 broadcast_in_dim.15
  9.7 0.1 convert_element_type.38
  9.8 0.1 broadcast_in_dim.34
  10.0 0.0 copy-done.8
  10.0 0.6 dynamic-slice
  11.2 0.0 copy-done.7
  11.2 0.2 dynamic-update-slice
  11.5 10.0 %all-reduce.2 = s32[1024]{0:T(1024)S(1)} all-reduce(s32[1024]{0:T(1024)S(1)} %dynamic-update-slice), channel_id=1, replica_groups=mesh['shot'=2,'col'=16] {'col'}, use_global_device_ids=true, to_apply=%add.2 | all-reduce | flops 1024 | bytes 8192
  21.5 0.7 iota_reduce_fusion
  22.2 0.0 collective-permute-done.1
  22.2 0.0 copy-done
  22.2 0.0 copy-start.2
  22.3 0.0 copy-start.3
  22.3 0.2 constant_dynamic-update-slice_fusion.1
  22.5 0.0 collective-permute-done
  22.6 0.9 copy-done.2
  23.5 0.3 copy-done.3
  23.8 2.4 %fusion.42 = f32[8,64,512]{2,1,0:T(8,128)S(1)} fusion(f32[8,64,512]{2,1,0:T(8,128)S(1)} %copy-done.2, f32[8,64,512]{2,1,0:T(8,128)S(1)} %copy-done, f32[12,64,512]{2,1,0:T(8,128)S(1)} %get-tuple-element.23, f32[12,64,512]{2,1,0:T(8,128)S(1)} %constant_dynamic-update-slice_fusion, f32[8,64,512]{2,1,0:T(8,128)S(1)} %copy-done.3, f32[64,512]{1,0:T(8,128)S(1)} %bitcast.22), kind=kLoop, calls=%fused_computation.88 | loop fusion | flops 8912896 | bytes 12713984 | tf_op jit(solution)/shard_map/mul | solution.py:61
  26.2 0.0 copy-start.1
  26.2 0.0 copy-start.4
  26.2 0.1 fusion.67
  26.3 6.3 %collective-permute-start.3 = (f32[4,64,512]{2,1,0:T(8,128)S(1)}, f32[4,64,512]{2,1,0:T(8,128)S(1)}, u32[]{:S(2)}, u32[]{:S(2)}) collective-permute-start(f32[4,64,512]{2,1,0:T(8,128)S(1)} %get-tuple-element.19), channel_id=1, source_target_pairs={{0,1},{1,2},{2,3},{3,4},{4,5},{5,6},{6,7},{7,8},{8,9},{9,10},{10,1... | collective-permute-start | bytes 1572872 | tf_op jit(solution)/shard_map/ppermute | solution.py:20
  32.6 4.8 %collective-permute-start.2 = (f32[4,64,512]{2,1,0:T(8,128)S(1)}, f32[4,64,512]{2,1,0:T(8,128)S(1)}, u32[]{:S(2)}, u32[]{:S(2)}) collective-permute-start(f32[4,64,512]{2,1,0:T(8,128)S(1)} %get-tuple-element.18), channel_id=1, source_target_pairs={{1,0},{2,1},{3,2},{4,3},{5,4},{6,5},{7,6},{8,7},{9,8},{10,9},{11,1... | collective-permute-start | bytes 1572872 | tf_op jit(solution)/shard_map/ppermute | solution.py:23
  37.4 0.2 convert_reduce_fusion.1
  37.6 1.1 %collective-permute-done.3 = f32[4,64,512]{2,1,0:T(8,128)S(1)} collective-permute-done((f32[4,64,512]{2,1,0:T(8,128)S(1)}, f32[4,64,512]{2,1,0:T(8,128)S(1)}, u32[]{:S(2)}, u32[]{:S(2)}) %collective-permute-start.3) | collective-permute-done | bytes 524320 | tf_op jit(solution)/shard_map/ppermute | solution.py:20
  38.7 4.4 %collective-permute-done.2 = f32[4,64,512]{2,1,0:T(8,128)S(1)} collective-permute-done((f32[4,64,512]{2,1,0:T(8,128)S(1)}, f32[4,64,512]{2,1,0:T(8,128)S(1)}, u32[]{:S(2)}, u32[]{:S(2)}) %collective-permute-start.2) | collective-permute-done | bytes 524320 | tf_op jit(solution)/shard_map/ppermute | solution.py:23
  43.1 0.0 copy-done.4
  43.1 5.2 %fusion.64 = (f32[8,64,512]{2,1,0:T(8,128)S(1)}, f32[8,64,512]{2,1,0:T(8,128)}) fusion(f32[8,64,512]{2,1,0:T(8,128)S(1)} %fusion.42, bf16[2,8,64,512]{3,2,1,0:T(8,128)(2,1)S(1)} %copy-done.4, f32[8,64,512]{2,1,0:T(8,128)S(1)} %copy-done.2, f32[4,64,512]{2,1,0:T(8,128)S(1)} %collective-permute-done.3, f32[4,64,512]{2,1,0:T(8,128)S(1)} %collective-permute-done.2, ...), kind=kLoop, calls=%fused_computation.117 | loop fusion | flops 12320768 | bytes 7471104 | tf_op jit(solution)/shard_map/add | solution.py:68
  48.3 0.4 reshape.43
  48.6 0.6 copy.16
  49.2 1.1 %broadcast_in_dim.35 = f32[64,8,4,128]{3,1,2,0:T(8,128)} broadcast(f32[]{:T(128)} %constant.50.clone.1), dimensions={} | broadcast | bytes 1048580 | tf_op jit(solution)/shard_map/broadcast_in_dim | solution.py:84
  50.4 8.1 %scatter_fusion = f32[64,8,4,128]{3,1,2,0:T(8,128)} fusion(f32[64,8,4,128]{3,1,2,0:T(8,128)} %broadcast_in_dim.35, s32[64]{0:T(128)S(1)} %compare_select_fusion.1, f32[64,8,4,128]{3,1,2,0:T(8,128)S(1)} %bitcast.19), kind=kCustom, calls=%fused_computation.1 | custom fusion | bytes 3145984 | tf_op jit(solution)/shard_map/scatter | solution.py:85
  58.5 9.2 %all-to-all-start = ((f32[64,8,4,128]{3,1,2,0:T(8,128)}), f32[64,8,4,128]{3,1,2,0:T(8,128)S(1)}, u32[]{:S(2)}, u32[]{:S(2)}) async-start(f32[64,8,4,128]{3,1,2,0:T(8,128)} %scatter_fusion), calls=%async_computation | async-start | bytes 2097152 | tf_op jit(solution)/shard_map/all_to_all | solution.py:86
  67.7 0.2 convert_reduce_fusion
  67.9 22.9 %all-to-all-done = f32[64,8,4,128]{3,1,2,0:T(8,128)S(1)} async-done(((f32[64,8,4,128]{3,1,2,0:T(8,128)}), f32[64,8,4,128]{3,1,2,0:T(8,128)S(1)}, u32[]{:S(2)}, u32[]{:S(2)}) %all-to-all-start) | async-done | bytes 1048608 | tf_op jit(solution)/shard_map/all_to_all | solution.py:86
  90.8 0.6 gather_fusion
  91.5 0.0 copy-done.5
  91.5 0.2 copy_add_fusion
  91.7 1.2 %copy.18 = f32[64,8,4,128]{3,2,1,0:T(4,128)} copy(f32[64,8,4,128]{3,1,2,0:T(8,128)S(1)} %copy_add_fusion) | data formatting | bytes 2097152
  (16 shorter events, 0.2 us)
Async XLA Ops:
  0.6 9.3 %copy-start.8 = (u32[32]{0:T(128)S(1)}, u32[32]{0:T(128)}, u32[]{:S(2)}) copy-start(u32[32]{0:T(128)} %constant.74) | copy-start | bytes 388
  0.6 21.6 %copy-start = (f32[8,64,512]{2,1,0:T(8,128)S(1)}, f32[8,64,512]{2,1,0:T(8,128)}, u32[]{:S(2)}) copy-start(f32[8,64,512]{2,1,0:T(8,128)} %param.8) | copy-start | bytes 3145732
  0.7 8.8 %copy-start.6 = (s32[2,64]{1,0:T(2,128)S(1)}, s32[2,64]{1,0:T(2,128)}, u32[]{:S(2)}) copy-start(s32[2,64]{1,0:T(2,128)} %param.11) | copy-start | bytes 1540
  0.7 10.6 %copy-start.7 = (s32[64]{0:T(128)S(1)}, s32[64]{0:T(128)}, u32[]{:S(2)}) copy-start(s32[64]{0:T(128)} %param.12) | copy-start | bytes 772
  3.0 19.2 %collective-permute-start.1 = (f32[4,64,512]{2,1,0:T(8,128)}, f32[4,64,512]{2,1,0:T(8,128)S(1)}, u32[]{:S(2)}, u32[]{:S(2)}) collective-permute-start(f32[4,64,512]{2,1,0:T(8,128)} %get-tuple-element.21), channel_id=1, source_target_pairs={{0,1},{1,2},{2,3},{3,4},{4,5},{5,6},{6,7},{7,8},{8,9},{9,10},{10,1... | collective-permute-start | bytes 1572872 | tf_op jit(solution)/shard_map/ppermute | solution.py:20
  7.5 15.0 %collective-permute-start = (f32[4,64,512]{2,1,0:T(8,128)}, f32[4,64,512]{2,1,0:T(8,128)S(1)}, u32[]{:S(2)}, u32[]{:S(2)}) collective-permute-start(f32[4,64,512]{2,1,0:T(8,128)} %get-tuple-element.20), channel_id=1, source_target_pairs={{1,0},{2,1},{3,2},{4,3},{5,4},{6,5},{7,6},{8,7},{9,8},{10,9},{11,1... | collective-permute-start | bytes 1572872 | tf_op jit(solution)/shard_map/ppermute | solution.py:23
  22.2 1.2 %copy-start.2 = (f32[8,64,512]{2,1,0:T(8,128)S(1)}, f32[8,64,512]{2,1,0:T(8,128)}, u32[]{:S(2)}) copy-start(f32[8,64,512]{2,1,0:T(8,128)} %param.9) | copy-start | bytes 3145732
  22.3 1.5 %copy-start.3 = (f32[8,64,512]{2,1,0:T(8,128)S(1)}, f32[8,64,512]{2,1,0:T(8,128)}, u32[]{:S(2)}) copy-start(f32[8,64,512]{2,1,0:T(8,128)} %param.7) | copy-start | bytes 3145732
  26.2 22.1 %copy-start.1 = (f32[8,64,512]{2,1,0:T(8,128)}, f32[8,64,512]{2,1,0:T(8,128)S(1)}, u32[]{:S(2)}) copy-start(f32[8,64,512]{2,1,0:T(8,128)S(1)} %fusion.42) | copy-start | bytes 3145732
  26.2 16.9 %copy-start.4 = (bf16[2,8,64,512]{3,2,1,0:T(8,128)(2,1)S(1)}, bf16[2,8,64,512]{3,2,1,0:T(8,128)(2,1)}, u32[]{:S(2)}) copy-start(bf16[2,8,64,512]{3,2,1,0:T(8,128)(2,1)} %param.10) | copy-start | bytes 3145732
  26.3 12.4 %collective-permute-start.3 = (f32[4,64,512]{2,1,0:T(8,128)S(1)}, f32[4,64,512]{2,1,0:T(8,128)S(1)}, u32[]{:S(2)}, u32[]{:S(2)}) collective-permute-start(f32[4,64,512]{2,1,0:T(8,128)S(1)} %get-tuple-element.19), channel_id=1, source_target_pairs={{0,1},{1,2},{2,3},{3,4},{4,5},{5,6},{6,7},{7,8},{8,9},{9,10},{10,1... | collective-permute-start | bytes 1572872 | tf_op jit(solution)/shard_map/ppermute | solution.py:20
  32.6 10.5 %collective-permute-start.2 = (f32[4,64,512]{2,1,0:T(8,128)S(1)}, f32[4,64,512]{2,1,0:T(8,128)S(1)}, u32[]{:S(2)}, u32[]{:S(2)}) collective-permute-start(f32[4,64,512]{2,1,0:T(8,128)S(1)} %get-tuple-element.18), channel_id=1, source_target_pairs={{1,0},{2,1},{3,2},{4,3},{5,4},{6,5},{7,6},{8,7},{9,8},{10,9},{11,1... | collective-permute-start | bytes 1572872 | tf_op jit(solution)/shard_map/ppermute | solution.py:23
  58.5 32.4 %all-to-all-start = ((f32[64,8,4,128]{3,1,2,0:T(8,128)}), f32[64,8,4,128]{3,1,2,0:T(8,128)S(1)}, u32[]{:S(2)}, u32[]{:S(2)}) async-start(f32[64,8,4,128]{3,1,2,0:T(8,128)} %scatter_fusion), calls=%async_computation | async-start | bytes 2097152 | tf_op jit(solution)/shard_map/all_to_all | solution.py:86
  67.7 23.8 %copy-start.5 = (f32[64,8,4,128]{3,2,1,0:T(4,128)S(1)}, f32[64,8,4,128]{3,2,1,0:T(4,128)}, u32[]{:S(2)}) copy-start(f32[64,8,4,128]{3,2,1,0:T(4,128)} %param.13) | copy-start | bytes 3145732
where the time goes:
time: 94.6 us; the launch traced here: 93 us
  waiting for transfers between devices  28.4 us (30%)
  starting transfers between devices  26.7 us (28%)
  local copies, waits for them, and re-layouts  17.3 us (18%)
  blocking collectives  9.98 us (11%)
  other arithmetic  8.93 us (9%)
  between operations  1.61 us (2%)
    all_to_all x1, waiting for transfers between devices, shards(): lax.all_to_all(outgoing, 'col', split_axis=0, concat_axis=0, tiled=True)  22.9 us
    ppermute x2, starting transfers between devices, with_halo(): lax.ppermute(lax.slice_in_dim(block, block.shape[dim] - width, None, axis...  10.8 us
    unnamed x1, blocking collectives  9.98 us
    all_to_all x1, starting transfers between devices, shards(): lax.all_to_all(outgoing, 'col', split_axis=0, concat_axis=0, tiled=True)  9.22 us
    scatter x1, local copies, waits for them, and re-layouts, shards(): outgoing = outgoing.at[target * capacity + send_rank].set(bricks)  8.14 us
    ppermute x2, starting transfers between devices, with_halo(): lax.ppermute(lax.slice_in_dim(block, 0, width, axis=dim), axis, backward)  6.69 us
    add x1, other arithmetic, shards(): source[0].astype(jnp.float32) * wave_first  5.18 us
    ppermute x2, waiting for transfers between devices, with_halo(): lax.ppermute(lax.slice_in_dim(block, 0, width, axis=dim), axis, backward)  4.4 us
  transfers between devices with their start and end apart: 5, of which 3 were waited for; matrix products, arithmetic and copies ran while one was open for 3% of the time, Pallas kernels for 0%

commit v1 on v0

v1 whole, which is shorter than its diff:
```python
import functools

import jax
import jax.numpy as jnp
from jax import lax
from jax.experimental import pallas as pl
from jax.experimental.pallas import tpu as pltpu
from jax.sharding import PartitionSpec as P

COEF = (-205.0 / 72.0, 8.0 / 5.0, -1.0 / 5.0, 8.0 / 315.0, -1.0 / 560.0)
MESH = pl.DeviceIdType.MESH
R = 4
PAD = 8
CH = 16
LANES = 128


def flipped(me, k, bits):
    out = me
    for b in range(bits):
        out = out + ((k // 2**b) % 2) * (2**b) * (1 - 2 * ((me // 2**b) % 2))
    return out


def kernel(
    n, cap, prev_h, now_h, vel_h, src_h, img_h, active_s, place_s, want_v,
    first_h, second_h, out_h,
    x1, x2, acc, prev_v, vel_v, src_v, img_v, second_v, bricks, outgoing, incoming, asked_v, asked_s,
    in_sem, halo_send, halo_recv, ask_send, ask_recv, ask_copy, a2a_send, a2a_recv, out_sem,
):
    me = lax.axis_index("col")
    cx, ny, nz = prev_h.shape
    n_c, n_z = ny // CH, nz // LANES
    slots = place_s.shape[0]
    bits = (n - 1).bit_length()

    def zero_rows(x, _):
        for j in range(n_z):
            for buf in (x1, x2):
                buf[R + x, j, 0:PAD, :] = jnp.zeros((PAD, LANES), jnp.float32)
                buf[R + x, j, PAD + ny : PAD + ny + PAD, :] = jnp.zeros((PAD, LANES), jnp.float32)
        return 0

    own = pl.ds(R, cx)
    body = pl.ds(PAD, ny)
    load_now = [
        pltpu.make_async_copy(
            now_h.at[:, :, pl.ds(j * LANES, LANES)], x1.at[own, j, body, :], in_sem.at[j]
        )
        for j in range(n_z)
    ]
    for copy in load_now:
        copy.start()
    load_prev = pltpu.make_async_copy(prev_h, prev_v, in_sem.at[n_z])
    load_vel = pltpu.make_async_copy(vel_h, vel_v, in_sem.at[n_z + 1])
    load_src = pltpu.make_async_copy(src_h, src_v, in_sem.at[n_z + 2])
    load_img = pltpu.make_async_copy(img_h, img_v, in_sem.at[n_z + 3])
    for copy in (load_prev, load_vel, load_src, load_img):
        copy.start()

    barrier = pltpu.get_barrier_semaphore()

    def greet(k, _):
        pl.semaphore_signal(
            barrier, inc=1, device_id={"col": lax.rem(me + k, n)}, device_id_type=MESH
        )
        return 0

    lax.fori_loop(1, n, greet, 0)

    lax.fori_loop(0, cx, zero_rows, 0)

    def zero_halo(start):
        def plane(x, _):
            for buf in (x1, x2):
                for j in range(n_z):
                    buf[start + x, j, PAD : PAD + ny, :] = jnp.zeros((ny, LANES), jnp.float32)
            return 0

        lax.fori_loop(0, R, plane, 0)

    @pl.when(me == 0)
    def _():
        zero_halo(0)

    @pl.when(me == n - 1)
    def _():
        zero_halo(R + cx)

    for copy in load_now:
        copy.wait()
    pl.semaphore_wait(barrier, n - 1)

    def halo(buf, step, side, c):
        rows = pl.ds(PAD + c * CH, CH)
        source, landing = ((cx, 0), (R, R + cx))[side]
        target = (lax.rem(me + 1, n), lax.rem(me + n - 1, n))[side]
        return pltpu.make_async_remote_copy(
            src_ref=buf.at[pl.ds(source, R), :, rows, :],
            dst_ref=buf.at[pl.ds(landing, R), :, rows, :],
            send_sem=halo_send.at[step, side, c],
            recv_sem=halo_recv.at[step, side, c],
            device_id={"col": target},
            device_id_type=MESH,
        )

    def send_halo(buf, step, c):
        @pl.when(me < n - 1)
        def _():
            halo(buf, step, 0, c).start()

        @pl.when(me > 0)
        def _():
            halo(buf, step, 1, c).start()

    def sent_halo(buf, step, c):
        @pl.when(me < n - 1)
        def _():
            halo(buf, step, 0, c).wait_send()

        @pl.when(me > 0)
        def _():
            halo(buf, step, 1, c).wait_send()

    def take_halo(buf, step, c):
        @pl.when(me > 0)
        def _():
            halo(buf, step, 0, c).wait_recv()

        @pl.when(me < n - 1)
        def _():
            halo(buf, step, 1, c).wait_recv()

    for c in range(n_c):
        send_halo(x1, 0, c)

    def ask(k):
        target = lax.rem(me + k, n)
        return pltpu.make_async_remote_copy(
            src_ref=want_v.at[target],
            dst_ref=asked_v.at[me],
            send_sem=ask_send,
            recv_sem=ask_recv,
            device_id={"col": target},
            device_id_type=MESH,
        )

    def start_ask(k, _):
        ask(k).start()
        return 0

    lax.fori_loop(1, n, start_ask, 0)
    asked_v[me] = want_v[me]

    lane = lax.broadcasted_iota(jnp.int32, (CH, LANES), 1)
    row = lax.broadcasted_iota(jnp.int32, (CH, LANES), 0)

    def along_yz(buf):
        def plane(x, _):
            for c in range(n_c):
                tiles = [buf[R + x, j, PAD + c * CH : PAD + (c + 1) * CH, :] for j in range(n_z)]
                for j in range(n_z):
                    total = (3.0 * COEF[0]) * tiles[j]
                    for r in range(1, R + 1):
                        at = PAD + c * CH
                        pair = buf[R + x, j, at + r : at + r + CH, :] + buf[R + x, j, at - r : at - r + CH, :]
                        up = pltpu.roll(tiles[j], LANES - r, 1)
                        down = pltpu.roll(tiles[j], r, 1)
                        after = pltpu.roll(tiles[j + 1], LANES - r, 1) if j + 1 < n_z else 0.0
                        before = pltpu.roll(tiles[j - 1], r, 1) if j > 0 else 0.0
                        pair = pair + jnp.where(lane < LANES - r, up, after)
                        pair = pair + jnp.where(lane < r, before, down)
                        total = total + COEF[r] * pair
                    acc[x, j, c * CH : (c + 1) * CH, :] = total
            return 0

        lax.fori_loop(0, cx, plane, 0)

    def mask(t, c, j):
        per = CH // 4
        flags = [active_s[t, (c * per + i) * n_z + j].astype(jnp.float32) for i in range(per)]
        out = jnp.full((CH, LANES), flags[per - 1], jnp.float32)
        for i in range(per - 2, -1, -1):
            out = jnp.where(row < 4 * (i + 1), flags[i], out)
        return out

    def following(buf, x, c, j, before, flag):
        rows = slice(PAD + c * CH, PAD + (c + 1) * CH)
        total = acc[x, j, c * CH : (c + 1) * CH, :]
        for r in range(1, R + 1):
            total = total + COEF[r] * (buf[R + x + r, j, rows, :] + buf[R + x - r, j, rows, :])
        here = buf[R + x, j, rows, :]
        speed = vel_v[x, c * CH : (c + 1) * CH, j * LANES : (j + 1) * LANES]
        return here, flag * (2.0 * here - before + speed * total)

    along_yz(x1)
    load_prev.wait()
    load_vel.wait()
    for c in range(n_c):
        take_halo(x1, 0, c)
        flags = [mask(0, c, j) for j in range(n_z)]

        def plane(x, _):
            for j in range(n_z):
                before = prev_v[x, c * CH : (c + 1) * CH, j * LANES : (j + 1) * LANES]
                _, new = following(x1, x, c, j, before, flags[j])
                x2[R + x, j, PAD + c * CH : PAD + (c + 1) * CH, :] = new
            return 0

        lax.fori_loop(0, cx, plane, 0)
        send_halo(x2, 1, c)

    store_first = [
        pltpu.make_async_copy(
            x2.at[own, j, body, :], first_h.at[:, :, pl.ds(j * LANES, LANES)], out_sem.at[j]
        )
        for j in range(n_z)
    ]
    for copy in store_first:
        copy.start()

    along_yz(x2)

    pltpu.make_async_copy(
        asked_v.at[pl.ds(0, n - 1)], asked_v.at[pl.ds(0, n - 1)], ask_recv
    ).wait()
    to_scalar = pltpu.make_async_copy(asked_v, asked_s, ask_copy)
    to_scalar.start()

    load_src.wait()
    for c in range(n_c):
        take_halo(x2, 1, c)
        flags = [mask(1, c, j) for j in range(n_z)]

        def pair(p, _):
            for j in range(n_z):
                gains = []
                for i in range(2):
                    x = 2 * p + i
                    before = x1[R + x, j, PAD + c * CH : PAD + (c + 1) * CH, :]
                    here, new = following(x2, x, c, j, before, flags[j])
                    spot = (slice(c * CH, (c + 1) * CH), slice(j * LANES, (j + 1) * LANES))
                    second_v[(x,) + spot] = new
                    gains.append(
                        src_v[(0, x) + spot].astype(jnp.float32) * here
                        + src_v[(1, x) + spot].astype(jnp.float32) * new
                    )
                for h in range(CH // 8):
                    a, b = (g[h * 8 : (h + 1) * 8, :] for g in gains)
                    low = row[:8] < 4
                    even = jnp.where(low, a, pltpu.roll(b, 4, 0))
                    odd = jnp.where(low, pltpu.roll(a, 4, 0), b)
                    yb = c * (CH // 4) + 2 * h
                    for i, value in enumerate((even, odd)):
                        bricks[(yb + i) * n_z + j, pl.ds(pl.multiple_of(8 * p, 8), 8), :] = value
            return 0

        lax.fori_loop(0, cx // 2, pair, 0)

    to_scalar.wait()

    def pack(dst, at, target):
        for r in range(cap):
            dst[at + r] = bricks[asked_s[target, 0, r]]

    def give(k, target):
        return pltpu.make_async_remote_copy(
            src_ref=outgoing.at[pl.ds(k * cap, cap)],
            dst_ref=incoming.at[pl.ds(me * cap, cap)],
            send_sem=a2a_send,
            recv_sem=a2a_recv,
            device_id={"col": target},
            device_id_type=MESH,
        )

    def partner(k):
        return flipped(me, k, bits) if n == 2**bits else lax.rem(me + k, n)

    def start_give(i, _):
        k = n - 1 - i
        target = partner(k)
        pack(outgoing, k * cap, target)
        give(k, target).start()
        return 0

    lax.fori_loop(0, n - 1, start_give, 0)

    store_second = pltpu.make_async_copy(second_v, second_h, out_sem.at[n_z])
    store_second.start()
    pack(incoming, me * cap, me)
    load_img.wait()

    whole = pl.ds(cap, (n - 1) * cap)
    pltpu.make_async_copy(incoming.at[whole], incoming.at[whole], a2a_recv).wait()
    parts = 4 if slots % 4 == 0 else 1
    per = slots // parts
    stores = []
    for q in range(parts):

        def add(s, _):
            at = q * per + s
            img_v[at] = img_v[at] + incoming[place_s[at]]
            return 0

        lax.fori_loop(0, per, add, 0)
        span = pl.ds(q * per, per)
        copy = pltpu.make_async_copy(img_v.at[span], out_h.at[span], out_sem.at[n_z + 1 + q])
        copy.start()
        stores.append(copy)

    for c in range(n_c):
        sent_halo(x1, 0, c)
        sent_halo(x2, 1, c)
    pltpu.make_async_copy(
        want_v.at[pl.ds(0, n - 1)], want_v.at[pl.ds(0, n - 1)], ask_send
    ).wait()
    pltpu.make_async_copy(outgoing.at[whole], outgoing.at[whole], a2a_send).wait()
    for copy in store_first + [store_second] + stores:
        copy.wait()


def shards(wave_prev, wave_now, velocity, source, active, plan, image_in):
    cx, ny, nz = wave_now.shape
    n = lax.axis_size("col")
    per = plan.shape[0]
    cap = (per + n - 1) // n
    n_c, n_z = ny // CH, nz // LANES

    order = jnp.arange(per, dtype=jnp.int32)
    anchor = lax.div(plan, jnp.int32(per))
    local = plan - anchor * per
    rank = jnp.sum(
        (anchor[None, :] == anchor[:, None]) & (order[None, :] < order[:, None]), axis=1, dtype=jnp.int32
    )
    place = anchor * cap + rank
    device = lax.broadcasted_iota(jnp.int32, (n, 1, LANES, per), 0)
    turn = lax.broadcasted_iota(jnp.int32, (n, 1, LANES, per), 2)
    hit = (anchor[None, None, None, :] == device) & (rank[None, None, None, :] == turn)
    want = jnp.sum(jnp.where(hit, local[None, None, None, :], 0), axis=3, dtype=jnp.int32)

    f32 = jnp.float32
    hbm = pl.BlockSpec(memory_space=pl.ANY)
    smem = pl.BlockSpec(memory_space=pltpu.SMEM)
    vmem = pl.BlockSpec(memory_space=pltpu.VMEM)
    wide = (cx + 2 * R, n_z, ny + 2 * PAD, LANES)
    dma = pltpu.SemaphoreType.DMA
    first, second, image = pl.pallas_call(
        functools.partial(kernel, n, cap),
        out_shape=(
            jax.ShapeDtypeStruct((cx, ny, nz), f32),
            jax.ShapeDtypeStruct((cx, ny, nz), f32),
            jax.ShapeDtypeStruct((per, 32, LANES), f32),
        ),
        in_specs=[hbm] * 5 + [smem, smem, vmem],
        out_specs=(hbm, hbm, hbm),
        scratch_shapes=[
            pltpu.VMEM(wide, f32),
            pltpu.VMEM(wide, f32),
            pltpu.VMEM((cx, n_z, ny, LANES), f32),
            pltpu.VMEM((cx, ny, nz), f32),
            pltpu.VMEM((cx, ny, nz), f32),
            pltpu.VMEM((2, cx, ny, nz), jnp.bfloat16),
            pltpu.VMEM((per, 32, LANES), f32),
            pltpu.VMEM((cx, ny, nz), f32),
            pltpu.VMEM((per, 32, LANES), f32),
            pltpu.VMEM((n * cap, 32, LANES), f32),
            pltpu.VMEM((n * cap, 32, LANES), f32),
            pltpu.VMEM((n, 1, LANES), jnp.int32),
            pltpu.SMEM((n, 1, LANES), jnp.int32),
            dma((n_z + 4,)),
            dma((2, 2, n_c)),
            dma((2, 2, n_c)),
            dma(()),
            dma(()),
            dma(()),
            dma(()),
            dma(()),
            dma((n_z + 5,)),
        ],
        compiler_params=pltpu.CompilerParams(
            collective_id=0, has_side_effects=True, vmem_limit_bytes=40 * 2**20
        ),
    )(
        wave_prev, wave_now, velocity, source, image_in.reshape(per, 32, LANES),
        active, place, want,
    )
    return first, second, image.reshape(image_in.shape)


def solution(mesh):
    lead = ("shot", "col")
    in_specs = (
        P(lead, None, None),
        P(lead, None, None),
        P(lead, None, None),
        P(None, lead, None, None),
        P(None, lead),
        P(lead),
        P(lead, None, None, None),
    )
    out_specs = (P(lead, None, None), P(lead, None, None), P(lead, None, None, None))
    return jax.shard_map(shards, mesh=mesh, in_specs=in_specs, out_specs=out_specs, check_vma=False)
```

time: 94.6 us -> 65.3 us (0.69); the launches traced: 93 us -> 65 us
  Pallas kernels: 0 us -> 53.6 us
  waiting for transfers between devices: 28.4 us -> 0 us
  starting transfers between devices: 26.7 us -> 0 us
  blocking collectives: 9.98 us -> 0 us
  other arithmetic: 8.93 us -> 0.33 us
  local copies, waits for them, and re-layouts: 17.3 us -> 10.4 us
    pallas_call x0 -> x1, Pallas kernels: none -> 53.6 us  [shards(): pl.pallas_call(functools.partial(kernel, n, cap), out_shape=(jax.ShapeDty...]
    all_to_all x1 -> x0, waiting for transfers between devices: 22.9 us -> none  [shards(): lax.all_to_all(outgoing, 'col', split_axis=0, concat_axis=0, tiled=True)]
    ppermute x4 -> x0, starting transfers between devices: 17.5 us -> none  [the longest x2 10.8 us: with_halo(): lax.ppermute(lax.slice_in_dim(block, block.shape[dim] - width, None, axis...]
    unnamed x1 -> x0, blocking collectives: 9.98 us -> none
    all_to_all x1 -> x0, starting transfers between devices: 9.22 us -> none  [shards(): lax.all_to_all(outgoing, 'col', split_axis=0, concat_axis=0, tiled=True)]
    scatter x1 -> x0, local copies, waits for them, and re-layouts: 8.14 us -> none  [shards(): outgoing = outgoing.at[target * capacity + send_rank].set(bricks)]
    unnamed x26 -> x17, local copies, waits for them, and re-layouts: 3.64 us -> 10.4 us
    ppermute x4 -> x0, waiting for transfers between devices: 5.52 us -> none  [the longest x2 4.4 us: with_halo(): lax.ppermute(lax.slice_in_dim(block, 0, width, axis=dim), axis, backward)]
  transfers between devices with their start and end apart: 5 -> 0, of which waited for: 3 -> 0; matrix products, arithmetic and copies ran while one was open for 3% -> 0% of each run, Pallas kernels for 0% -> 0%
where the time goes in v1:
time: 65.3 us; the launch traced here: 65 us
  Pallas kernels  53.6 us (82%)
  local copies, waits for them, and re-layouts  10.4 us (16%)
  between operations  0.67 us (1%)
    pallas_call x1, Pallas kernels, shards(): pl.pallas_call(functools.partial(kernel, n, cap), out_shape=(jax.ShapeDty...  53.6 us
    unnamed x17, local copies, waits for them, and re-layouts  10.4 us

profile of v1, /device:TPU:1, one launch (start us, length us, event | category | flops | bytes accessed | tf_op | source)
XLA Modules:
  0.0 65.0 jit_solution(404390384866347001)
XLA Ops:
  0.6 0.0 copy-start.6
  0.6 0.6 copy-done.6
  1.3 0.2 convert_reduce_fusion
  1.5 0.1 select_reduce_fusion
  1.6 0.0 copy-start.5
  1.6 0.7 %copy-done.5 = s32[2,64]{1,0:T(2,128)S(1)} copy-done((s32[2,64]{1,0:T(2,128)S(1)}, s32[2,64]{1,0:T(2,128)}, u32[]{:S(2)}) %copy-start.5) | copy-done | bytes 536
  2.3 0.0 copy-start
  2.3 1.2 %copy-done = f32[8,64,512]{2,1,0:T(8,128)S(1)} copy-done((f32[8,64,512]{2,1,0:T(8,128)S(1)}, f32[8,64,512]{2,1,0:T(8,128)}, u32[]{:S(2)}) %copy-start) | copy-done | bytes 1048600
  3.5 0.0 copy-start.1
  3.5 1.2 %copy-done.1 = f32[8,64,512]{2,1,0:T(8,128)S(1)} copy-done((f32[8,64,512]{2,1,0:T(8,128)S(1)}, f32[8,64,512]{2,1,0:T(8,128)}, u32[]{:S(2)}) %copy-start.1) | copy-done | bytes 1048600
  4.8 0.0 copy-start.2
  4.8 1.2 %copy-done.2 = f32[8,64,512]{2,1,0:T(8,128)S(1)} copy-done((f32[8,64,512]{2,1,0:T(8,128)S(1)}, f32[8,64,512]{2,1,0:T(8,128)}, u32[]{:S(2)}) %copy-start.2) | copy-done | bytes 1048600
  6.0 0.0 copy-start.3
  6.0 1.2 %copy-done.3 = bf16[2,8,64,512]{3,2,1,0:T(8,128)(2,1)S(1)} copy-done((bf16[2,8,64,512]{3,2,1,0:T(8,128)(2,1)S(1)}, bf16[2,8,64,512]{3,2,1,0:T(8,128)(2,1)}, u32[]{:S(2)}) %copy-start.3) | copy-done | bytes 1048600
  7.2 0.0 copy-start.4
  7.2 1.2 %copy-done.4 = f32[64,8,4,128]{3,2,1,0:T(4,128)S(1)} copy-done((f32[64,8,4,128]{3,2,1,0:T(4,128)S(1)}, f32[64,8,4,128]{3,2,1,0:T(4,128)}, u32[]{:S(2)}) %copy-start.4) | copy-done | bytes 1048600
  8.4 53.6 %shard_map.99 = (f32[8,64,512]{2,1,0:T(8,128)S(1)}, f32[8,64,512]{2,1,0:T(8,128)S(1)}, f32[64,32,128]{2,1,0:T(8,128)S(1)}) custom-call(f32[8,64,512]{2,1,0:T(8,128)S(1)} %copy-done, f32[8,64,512]{2,1,0:T(8,128)S(1)} %copy-done.1, f32[8,64,512]{2,1,0:T(8,128)S(1)} %copy-done.2, bf16[2,8,64,512]{3,2,1,0:T(8,128)(2,1)S(1)} %copy-done.3, ...), custom_call_target="tpu_custom_call" | custom-call | tf_op jit(solution)/shard_map/pallas_call | solution.py:347
  62.1 1.0 %copy.13 = f32[8,64,512]{2,1,0:T(8,128)} copy(f32[8,64,512]{2,1,0:T(8,128)S(1)} %get-tuple-element.14) | data formatting | bytes 2097152
  63.0 1.0 %copy.14 = f32[8,64,512]{2,1,0:T(8,128)} copy(f32[8,64,512]{2,1,0:T(8,128)S(1)} %get-tuple-element.15) | data formatting | bytes 2097152
  64.0 1.0 %copy.15 = f32[64,8,4,128]{3,2,1,0:T(4,128)} copy(f32[64,8,4,128]{3,2,1,0:T(4,128)S(1)} %bitcast.3) | data formatting | bytes 2097152
  (2 shorter events, 0.0 us)
Async XLA Ops:
  0.6 0.7 %copy-start.6 = (s32[64]{0:T(128)S(1)}, s32[64]{0:T(128)}, u32[]{:S(2)}) copy-start(s32[64]{0:T(128)} %param.12) | copy-start | bytes 772
  1.6 0.7 %copy-start.5 = (s32[2,64]{1,0:T(2,128)S(1)}, s32[2,64]{1,0:T(2,128)}, u32[]{:S(2)}) copy-start(s32[2,64]{1,0:T(2,128)} %active_s.1) | copy-start | bytes 1540
  2.3 1.2 %copy-start = (f32[8,64,512]{2,1,0:T(8,128)S(1)}, f32[8,64,512]{2,1,0:T(8,128)}, u32[]{:S(2)}) copy-start(f32[8,64,512]{2,1,0:T(8,128)} %prev_h.1) | copy-start | bytes 3145732
  3.5 1.2 %copy-start.1 = (f32[8,64,512]{2,1,0:T(8,128)S(1)}, f32[8,64,512]{2,1,0:T(8,128)}, u32[]{:S(2)}) copy-start(f32[8,64,512]{2,1,0:T(8,128)} %now_h.1) | copy-start | bytes 3145732
  4.8 1.2 %copy-start.2 = (f32[8,64,512]{2,1,0:T(8,128)S(1)}, f32[8,64,512]{2,1,0:T(8,128)}, u32[]{:S(2)}) copy-start(f32[8,64,512]{2,1,0:T(8,128)} %vel_h.1) | copy-start | bytes 3145732
  6.0 1.2 %copy-start.3 = (bf16[2,8,64,512]{3,2,1,0:T(8,128)(2,1)S(1)}, bf16[2,8,64,512]{3,2,1,0:T(8,128)(2,1)}, u32[]{:S(2)}) copy-start(bf16[2,8,64,512]{3,2,1,0:T(8,128)(2,1)} %src_h.1) | copy-start | bytes 3145732
  7.2 1.2 %copy-start.4 = (f32[64,8,4,128]{3,2,1,0:T(4,128)S(1)}, f32[64,8,4,128]{3,2,1,0:T(4,128)}, u32[]{:S(2)}) copy-start(f32[64,8,4,128]{3,2,1,0:T(4,128)} %param.13) | copy-start | bytes 3145732

commit v2 on v1

--- a/solution.py
+++ b/solution.py
@@ -23,15 +23,14 @@
 
 
 def kernel(
-    n, cap, prev_h, now_h, vel_h, src_h, img_h, active_s, place_s, want_v,
-    first_h, second_h, out_h,
-    x1, x2, acc, prev_v, vel_v, src_v, img_v, second_v, bricks, outgoing, incoming, asked_v, asked_s,
-    in_sem, halo_send, halo_recv, ask_send, ask_recv, ask_copy, a2a_send, a2a_recv, out_sem,
+    n, cap, prev_h, now_h, vel_h, src_h, active_s, want_v,
+    first_h, second_h, incoming,
+    x1, x2, acc, prev_v, vel_v, src_v, second_v, bricks, outgoing, asked_v, asked_s,
+    in_sem, halo_send, halo_recv, ask_send, ask_recv, ask_copy, a2a_send, a2a_recv, keep_sem, out_sem,
 ):
     me = lax.axis_index("col")
     cx, ny, nz = prev_h.shape
     n_c, n_z = ny // CH, nz // LANES
-    slots = place_s.shape[0]
     bits = (n - 1).bit_length()
 
     def zero_rows(x, _):
@@ -54,8 +53,7 @@
     load_prev = pltpu.make_async_copy(prev_h, prev_v, in_sem.at[n_z])
     load_vel = pltpu.make_async_copy(vel_h, vel_v, in_sem.at[n_z + 1])
     load_src = pltpu.make_async_copy(src_h, src_v, in_sem.at[n_z + 2])
-    load_img = pltpu.make_async_copy(img_h, img_v, in_sem.at[n_z + 3])
-    for copy in (load_prev, load_vel, load_src, load_img):
+    for copy in (load_prev, load_vel, load_src):
         copy.start()
 
     barrier = pltpu.get_barrier_semaphore()
@@ -287,26 +285,14 @@
 
     store_second = pltpu.make_async_copy(second_v, second_h, out_sem.at[n_z])
     store_second.start()
-    pack(incoming, me * cap, me)
-    load_img.wait()
+    pack(outgoing, 0, me)
+    keep = pltpu.make_async_copy(
+        outgoing.at[pl.ds(0, cap)], incoming.at[pl.ds(me * cap, cap)], keep_sem
+    )
+    keep.start()
 
     whole = pl.ds(cap, (n - 1) * cap)
     pltpu.make_async_copy(incoming.at[whole], incoming.at[whole], a2a_recv).wait()
-    parts = 4 if slots % 4 == 0 else 1
-    per = slots // parts
-    stores = []
-    for q in range(parts):
-
-        def add(s, _):
-            at = q * per + s
-            img_v[at] = img_v[at] + incoming[place_s[at]]
-            return 0
-
-        lax.fori_loop(0, per, add, 0)
-        span = pl.ds(q * per, per)
-        copy = pltpu.make_async_copy(img_v.at[span], out_h.at[span], out_sem.at[n_z + 1 + q])
-        copy.start()
-        stores.append(copy)
 
     for c in range(n_c):
         sent_halo(x1, 0, c)
@@ -315,7 +301,44 @@
         want_v.at[pl.ds(0, n - 1)], want_v.at[pl.ds(0, n - 1)], ask_send
     ).wait()
     pltpu.make_async_copy(outgoing.at[whole], outgoing.at[whole], a2a_send).wait()
-    for copy in store_first + [store_second] + stores:
+    for copy in store_first + [store_second, keep]:
+        copy.wait()
+
+
+def finish(
+    place_s, first_h, second_h, incoming_h, img_h, first_out, second_out, image_out,
+    incoming, img_v, sum_v, sem,
+):
+    loads = [
+        pltpu.make_async_copy(incoming_h, incoming, sem.at[6]),
+        pltpu.make_async_copy(img_h, img_v, sem.at[7]),
+    ]
+    for copy in loads:
+        copy.start()
+    copies = [
+        pltpu.make_async_copy(first_h, first_out, sem.at[0]),
+        pltpu.make_async_copy(second_h, second_out, sem.at[1]),
+    ]
+    for copy in copies:
+        copy.start()
+    per = place_s.shape[0]
+    parts = 4 if per % 4 == 0 else 1
+    step = per // parts
+    for copy in loads:
+        copy.wait()
+    for q in range(parts):
+
+        def add(i, _):
+            s = q * step + i
+            sum_v[s] = img_v[s] + incoming[place_s[s]]
+            return 0
+
+        lax.fori_loop(0, step, add, 0)
+        span = pl.ds(q * step, step)
+        copy = pltpu.make_async_copy(sum_v.at[span], image_out.at[span], sem.at[2 + q])
+        copy.start()
+        copies.append(copy)
+    for copy in copies:
         copy.wait()
 
 
@@ -339,20 +362,21 @@
     want = jnp.sum(jnp.where(hit, local[None, None, None, :], 0), axis=3, dtype=jnp.int32)
 
     f32 = jnp.float32
-    hbm = pl.BlockSpec(memory_space=pl.ANY)
+    hbm = pl.BlockSpec(memory_space=pltpu.HBM)
+    free = pl.BlockSpec(memory_space=pl.ANY)
     smem = pl.BlockSpec(memory_space=pltpu.SMEM)
     vmem = pl.BlockSpec(memory_space=pltpu.VMEM)
     wide = (cx + 2 * R, n_z, ny + 2 * PAD, LANES)
     dma = pltpu.SemaphoreType.DMA
-    first, second, image = pl.pallas_call(
+    first, second, incoming = pl.pallas_call(
         functools.partial(kernel, n, cap),
         out_shape=(
             jax.ShapeDtypeStruct((cx, ny, nz), f32),
             jax.ShapeDtypeStruct((cx, ny, nz), f32),
-            jax.ShapeDtypeStruct((per, 32, LANES), f32),
+            jax.ShapeDtypeStruct((n * cap, 32, LANES), f32),
         ),
-        in_specs=[hbm] * 5 + [smem, smem, vmem],
-        out_specs=(hbm, hbm, hbm),
+        in_specs=[hbm] * 4 + [smem, vmem],
+        out_specs=(free, free, free),
         scratch_shapes=[
             pltpu.VMEM(wide, f32),
             pltpu.VMEM(wide, f32),
@@ -360,14 +384,12 @@
             pltpu.VMEM((cx, ny, nz), f32),
             pltpu.VMEM((cx, ny, nz), f32),
             pltpu.VMEM((2, cx, ny, nz), jnp.bfloat16),
-            pltpu.VMEM((per, 32, LANES), f32),
             pltpu.VMEM((cx, ny, nz), f32),
             pltpu.VMEM((per, 32, LANES), f32),
             pltpu.VMEM((n * cap, 32, LANES), f32),
-            pltpu.VMEM((n * cap, 32, LANES), f32),
             pltpu.VMEM((n, 1, LANES), jnp.int32),
             pltpu.SMEM((n, 1, LANES), jnp.int32),
-            dma((n_z + 4,)),
+            dma((n_z + 3,)),
             dma((2, 2, n_c)),
             dma((2, 2, n_c)),
             dma(()),
@@ -375,15 +397,32 @@
             dma(()),
             dma(()),
             dma(()),
-            dma((n_z + 5,)),
+            dma(()),
+            dma((n_z + 1,)),
         ],
         compiler_params=pltpu.CompilerParams(
-            collective_id=0, has_side_effects=True, vmem_limit_bytes=40 * 2**20
+            collective_id=0, has_side_effects=True, vmem_limit_bytes=60 * 2**20
         ),
     )(
-        wave_prev, wave_now, velocity, source, image_in.reshape(per, 32, LANES),
-        active, place, want,
+        wave_prev, wave_now, velocity, source, active, want
     )
+    first, second, image = pl.pallas_call(
+        finish,
+        out_shape=(
+            jax.ShapeDtypeStruct((cx, ny, nz), f32),
+            jax.ShapeDtypeStruct((cx, ny, nz), f32),
+            jax.ShapeDtypeStruct((per, 32, LANES), f32),
+        ),
+        in_specs=[smem, free, free, free, free],
+        out_specs=(hbm, hbm, hbm),
+        scratch_shapes=[
+            pltpu.VMEM((n * cap, 32, LANES), f32),
+            pltpu.VMEM((per, 32, LANES), f32),
+            pltpu.VMEM((per, 32, LANES), f32),
+            dma((8,)),
+        ],
+        compiler_params=pltpu.CompilerParams(vmem_limit_bytes=60 * 2**20),
+    )(place, first, second, incoming, image_in.reshape(per, 32, LANES))
     return first, second, image.reshape(image_in.shape)
 
 

time: 65.3 us -> 121 us (1.85)
  Pallas kernels: 53.6 us -> 118 us
  local copies, waits for them, and re-layouts: 10.4 us -> 0.65 us
    pallas_call x0 -> x1, Pallas kernels: none -> 65.4 us  [shards(): pl.pallas_call(finish, out_shape=(jax.ShapeDtypeStruct((cx, ny, nz), f32)...]
    unnamed x17 -> x2, local copies, waits for them, and re-layouts: 10.4 us -> 0.65 us
where the time goes in v2:
time: 121 us
  Pallas kernels  118 us (98%)
  other arithmetic  1.41 us (1%)
    pallas_call x1, Pallas kernels, shards(): pl.pallas_call(finish, out_shape=(jax.ShapeDtypeStruct((cx, ny, nz), f32)...  65.4 us
    pallas_call x1, Pallas kernels, shards(): pl.pallas_call(functools.partial(kernel, n, cap), out_shape=(jax.ShapeDty...  53.1 us

profile of v2, /device:TPU:1, one launch (start us, length us, event | category | flops | bytes accessed | tf_op | source)
XLA Modules:
  0.0 121.2 jit_solution(17589324534078608060)
XLA Ops:
  0.6 0.0 copy-start
  0.6 0.6 copy-done
  1.3 0.2 convert_reduce_fusion
  1.5 0.5 multiply_add_fusion.place_s
  2.0 0.7 select_reduce_fusion
  2.7 53.1 %shard_map.99 = (f32[8,64,512]{2,1,0:T(8,128)}, f32[8,64,512]{2,1,0:T(8,128)}, f32[64,32,128]{2,1,0:T(8,128)}) custom-call(f32[8,64,512]{2,1,0:T(8,128)} %prev_h.1, f32[8,64,512]{2,1,0:T(8,128)} %now_h.1, f32[8,64,512]{2,1,0:T(8,128)} %vel_h.1, bf16[2,8,64,512]{3,2,1,0:T(8,128)(2,1)} %src_h.1, s32[2,64]{1,0:T(2,128)} %active_s.1, s32[16,1,128]{2,1,0:T(1,128)} %bitcast.4), custom_call_target="tpu_custom_call" | custom-call | tf_op jit(solution)/shard_map/pallas_call | solution.py:371
  55.8 65.4 %shard_map.100 = (f32[8,64,512]{2,1,0:T(8,128)}, f32[8,64,512]{2,1,0:T(8,128)}, f32[64,32,128]{2,1,0:T(8,128)}) custom-call(s32[64]{0:T(128)} %multiply_add_fusion.place_s, f32[8,64,512]{2,1,0:T(8,128)} %get-tuple-element.9.first_h, f32[8,64,512]{2,1,0:T(8,128)} %get-tuple-element.10.second_h, f32[64,32,128]{2,1,0:T(8,128)} %get-tuple-element.11.incoming_h, ...), custom_call_target="tpu_custom_call" | custom-call | tf_op jit(solution)/shard_map/pallas_call | solution.py:409
  (1 shorter events, 0.0 us)
Async XLA Ops:
  0.6 0.7 copy-start

commit v3 on v2

--- a/solution.py
+++ b/solution.py
@@ -23,9 +23,9 @@
 
 
 def kernel(
-    n, cap, prev_h, now_h, vel_h, src_h, active_s, want_v,
-    first_h, second_h, incoming,
-    x1, x2, acc, prev_v, vel_v, src_v, second_v, bricks, outgoing, asked_v, asked_s,
+    n, cap, prev_h, now_h, vel_h, src_h, active_h, plan_h,
+    first_h, second_h, incoming, place_v,
+    x1, x2, acc, prev_v, vel_v, src_v, second_v, bricks, outgoing, active_s, plan_s, want_2d, want_v, asked_v, asked_s,
     in_sem, halo_send, halo_recv, ask_send, ask_recv, ask_copy, a2a_send, a2a_recv, keep_sem, out_sem,
 ):
     me = lax.axis_index("col")
@@ -50,6 +50,10 @@
     ]
     for copy in load_now:
         copy.start()
+    load_plan = pltpu.make_async_copy(plan_h, plan_s, in_sem.at[n_z + 3])
+    load_active = pltpu.make_async_copy(active_h, active_s, in_sem.at[n_z + 4])
+    load_plan.start()
+    load_active.start()
     load_prev = pltpu.make_async_copy(prev_h, prev_v, in_sem.at[n_z])
     load_vel = pltpu.make_async_copy(vel_h, vel_v, in_sem.at[n_z + 1])
     load_src = pltpu.make_async_copy(src_h, src_v, in_sem.at[n_z + 2])
@@ -131,6 +135,45 @@
 
     for c in range(n_c):
         send_halo(x1, 0, c)
+
+    load_plan.wait()
+    load_active.wait()
+    per = plan_s.shape[0]
+    slot = lax.broadcasted_iota(jnp.int32, (8, LANES), 1)
+    zero = jnp.zeros((8, LANES), jnp.int32)
+
+    def spread(s, carry):
+        anchor, local = carry
+        device = lax.div(plan_s[s], per)
+        here = slot == s
+        return jnp.where(here, device, anchor), jnp.where(here, plan_s[s] - device * per, local)
+
+    anchor, local = lax.fori_loop(0, per, spread, (zero - 1, zero), unroll=8)
+
+    def count(s, rank):
+        device = lax.div(plan_s[s], per)
+        return rank + jnp.where((slot > s) & (anchor == device), 1, 0)
+
+    rank = lax.fori_loop(0, per, count, zero, unroll=8)
+    place_v[...] = (anchor * cap + rank)[:1]
+
+    def table(i, _):
+        device = lax.broadcasted_iota(jnp.int32, (8, LANES), 0) + 8 * i
+        rows = zero
+        for r in range(cap):
+            hit = (anchor == device) & (rank == r)
+            pick = jnp.sum(jnp.where(hit, local, 0), axis=1, keepdims=True)
+            rows = jnp.where(slot == r, pick, rows)
+        want_2d[pl.ds(pl.multiple_of(8 * i, 8), 8), :] = rows
+        return 0
+
+    lax.fori_loop(0, (n + 7) // 8, table, 0)
+
+    def lay(k, _):
+        want_v[k] = want_2d[pl.ds(k, 1), :]
+        return 0
+
+    lax.fori_loop(0, n, lay, 0)
 
     def ask(k):
         target = lax.rem(me + k, n)
@@ -307,21 +350,26 @@
 
 def finish(
     place_s, first_h, second_h, incoming_h, img_h, first_out, second_out, image_out,
-    incoming, img_v, sum_v, sem,
+    first_v, second_v, incoming, img_v, sum_v, sem,
 ):
+    waves = [
+        pltpu.make_async_copy(first_h, first_v, sem.at[8]),
+        pltpu.make_async_copy(second_h, second_v, sem.at[9]),
+    ]
     loads = [
         pltpu.make_async_copy(incoming_h, incoming, sem.at[6]),
         pltpu.make_async_copy(img_h, img_v, sem.at[7]),
     ]
-    for copy in loads:
+    for copy in waves + loads:
         copy.start()
     copies = [
-        pltpu.make_async_copy(first_h, first_out, sem.at[0]),
-        pltpu.make_async_copy(second_h, second_out, sem.at[1]),
+        pltpu.make_async_copy(first_v, first_out, sem.at[0]),
+        pltpu.make_async_copy(second_v, second_out, sem.at[1]),
     ]
-    for copy in copies:
-        copy.start()
-    per = place_s.shape[0]
+    for load, copy in zip(waves, copies):
+        load.wait()
+        copy.start()
+    per = img_v.shape[0]
     parts = 4 if per % 4 == 0 else 1
     step = per // parts
     for copy in loads:
@@ -330,7 +378,7 @@
 
         def add(i, _):
             s = q * step + i
-            sum_v[s] = img_v[s] + incoming[place_s[s]]
+            sum_v[s] = img_v[s] + incoming[place_s[0, s]]
             return 0
 
         lax.fori_loop(0, step, add, 0)
@@ -349,34 +397,24 @@
     cap = (per + n - 1) // n
     n_c, n_z = ny // CH, nz // LANES
 
-    order = jnp.arange(per, dtype=jnp.int32)
-    anchor = lax.div(plan, jnp.int32(per))
-    local = plan - anchor * per
-    rank = jnp.sum(
-        (anchor[None, :] == anchor[:, None]) & (order[None, :] < order[:, None]), axis=1, dtype=jnp.int32
-    )
-    place = anchor * cap + rank
-    device = lax.broadcasted_iota(jnp.int32, (n, 1, LANES, per), 0)
-    turn = lax.broadcasted_iota(jnp.int32, (n, 1, LANES, per), 2)
-    hit = (anchor[None, None, None, :] == device) & (rank[None, None, None, :] == turn)
-    want = jnp.sum(jnp.where(hit, local[None, None, None, :], 0), axis=3, dtype=jnp.int32)
-
     f32 = jnp.float32
     hbm = pl.BlockSpec(memory_space=pltpu.HBM)
     free = pl.BlockSpec(memory_space=pl.ANY)
     smem = pl.BlockSpec(memory_space=pltpu.SMEM)
     vmem = pl.BlockSpec(memory_space=pltpu.VMEM)
+    assert per <= LANES
     wide = (cx + 2 * R, n_z, ny + 2 * PAD, LANES)
     dma = pltpu.SemaphoreType.DMA
-    first, second, incoming = pl.pallas_call(
+    first, second, incoming, place = pl.pallas_call(
         functools.partial(kernel, n, cap),
         out_shape=(
             jax.ShapeDtypeStruct((cx, ny, nz), f32),
             jax.ShapeDtypeStruct((cx, ny, nz), f32),
             jax.ShapeDtypeStruct((n * cap, 32, LANES), f32),
+            jax.ShapeDtypeStruct((1, LANES), jnp.int32),
         ),
-        in_specs=[hbm] * 4 + [smem, vmem],
-        out_specs=(free, free, free),
+        in_specs=[hbm] * 6,
+        out_specs=(free, free, free, vmem),
         scratch_shapes=[
             pltpu.VMEM(wide, f32),
             pltpu.VMEM(wide, f32),
@@ -387,9 +425,13 @@
             pltpu.VMEM((cx, ny, nz), f32),
             pltpu.VMEM((per, 32, LANES), f32),
             pltpu.VMEM((n * cap, 32, LANES), f32),
+            pltpu.SMEM(active.shape, jnp.int32),
+            pltpu.SMEM((per,), jnp.int32),
+            pltpu.VMEM(((n + 7) // 8 * 8, LANES), jnp.int32),
+            pltpu.VMEM((n, 1, LANES), jnp.int32),
             pltpu.VMEM((n, 1, LANES), jnp.int32),
             pltpu.SMEM((n, 1, LANES), jnp.int32),
-            dma((n_z + 3,)),
+            dma((n_z + 5,)),
             dma((2, 2, n_c)),
             dma((2, 2, n_c)),
             dma(()),
@@ -404,7 +446,7 @@
             collective_id=0, has_side_effects=True, vmem_limit_bytes=60 * 2**20
         ),
     )(
-        wave_prev, wave_now, velocity, source, active, want
+        wave_prev, wave_now, velocity, source, active, plan
     )
     first, second, image = pl.pallas_call(
         finish,
@@ -416,10 +458,12 @@
         in_specs=[smem, free, free, free, free],
         out_specs=(hbm, hbm, hbm),
         scratch_shapes=[
+            pltpu.VMEM((cx, ny, nz), f32),
+            pltpu.VMEM((cx, ny, nz), f32),
             pltpu.VMEM((n * cap, 32, LANES), f32),
             pltpu.VMEM((per, 32, LANES), f32),
             pltpu.VMEM((per, 32, LANES), f32),
-            dma((8,)),
+            dma((10,)),
         ],
         compiler_params=pltpu.CompilerParams(vmem_limit_bytes=60 * 2**20),
     )(place, first, second, incoming, image_in.reshape(per, 32, LANES))

time: 121 us -> 58 us (0.48)
  Pallas kernels: 118 us -> 57.2 us
  other arithmetic: 1.41 us -> 0 us
    pallas_call x1, Pallas kernels: 65.4 us -> 4.13 us  [shards(): pl.pallas_call(finish, out_shape=(jax.ShapeDtypeStruct((cx, ny, nz), f32)...]
where the time goes in v3:
time: 58 us; the launch traced here: 57.8 us
  Pallas kernels  57.2 us (99%)
  between operations  0.64 us (1%)
    pallas_call x1, Pallas kernels, shards(): pl.pallas_call(functools.partial(kernel, n, cap), out_shape=(jax.ShapeDty...  53.1 us
    pallas_call x1, Pallas kernels, shards(): pl.pallas_call(finish, out_shape=(jax.ShapeDtypeStruct((cx, ny, nz), f32)...  4.13 us

profile of v3, /device:TPU:1, one launch (start us, length us, event | category | flops | bytes accessed | tf_op | source)
XLA Modules:
  0.0 57.8 jit_solution(6824505293765907262)
XLA Ops:
  0.6 53.1 %shard_map.94 = (f32[8,64,512]{2,1,0:T(8,128)}, f32[8,64,512]{2,1,0:T(8,128)}, f32[64,32,128]{2,1,0:T(8,128)}, s32[1,128]{1,0:T(1,128)}) custom-call(f32[8,64,512]{2,1,0:T(8,128)} %prev_h.1, f32[8,64,512]{2,1,0:T(8,128)} %now_h.1, f32[8,64,512]{2,1,0:T(8,128)} %vel_h.1, bf16[2,8,64,512]{3,2,1,0:T(8,128)(2,1)} %src_h.1, s32[2,64]{1,0:T(2,128)} %active_h.1, ...), custom_call_target="tpu_custom_call" | custom-call | tf_op jit(solution)/shard_map/pallas_call | solution.py:408
  53.7 4.1 %shard_map.95 = (f32[8,64,512]{2,1,0:T(8,128)}, f32[8,64,512]{2,1,0:T(8,128)}, f32[64,32,128]{2,1,0:T(8,128)}) custom-call(s32[1,128]{1,0:T(1,128)} %get-tuple-element.10.place_s, f32[8,64,512]{2,1,0:T(8,128)} %get-tuple-element.11.first_h, f32[8,64,512]{2,1,0:T(8,128)} %get-tuple-element.12.second_h, f32[64,32,128]{2,1,0:T(8,128)} %get-tuple-element.13.incoming_h, ...), custom_call_target="tpu_custom_call" | custom-call | tf_op jit(solution)/shard_map/pallas_call | solution.py:451

commit v4 on v3

--- a/solution.py
+++ b/solution.py
@@ -234,6 +234,26 @@
         speed = vel_v[x, c * CH : (c + 1) * CH, j * LANES : (j + 1) * LANES]
         return here, flag * (2.0 * here - before + speed * total)
 
+    even = lax.rem(me, 2) == 0
+
+    def take_near(buf, step, c):
+        @pl.when(jnp.logical_not(even))
+        def _():
+            halo(buf, step, 0, c).wait_recv()
+
+        @pl.when(even & (me < n - 1))
+        def _():
+            halo(buf, step, 1, c).wait_recv()
+
+    def take_other(buf, step, c):
+        @pl.when(even & (me > 0))
+        def _():
+            halo(buf, step, 0, c).wait_recv()
+
+        @pl.when(jnp.logical_not(even) & (me < n - 1))
+        def _():
+            halo(buf, step, 1, c).wait_recv()
+
     along_yz(x1)
     load_prev.wait()
     load_vel.wait()
@@ -269,70 +289,105 @@
     to_scalar.start()
 
     load_src.wait()
-    for c in range(n_c):
-        take_halo(x2, 1, c)
-        flags = [mask(1, c, j) for j in range(n_z)]
-
-        def pair(p, _):
-            for j in range(n_z):
-                gains = []
-                for i in range(2):
-                    x = 2 * p + i
-                    before = x1[R + x, j, PAD + c * CH : PAD + (c + 1) * CH, :]
-                    here, new = following(x2, x, c, j, before, flags[j])
-                    spot = (slice(c * CH, (c + 1) * CH), slice(j * LANES, (j + 1) * LANES))
-                    second_v[(x,) + spot] = new
-                    gains.append(
-                        src_v[(0, x) + spot].astype(jnp.float32) * here
-                        + src_v[(1, x) + spot].astype(jnp.float32) * new
-                    )
-                for h in range(CH // 8):
-                    a, b = (g[h * 8 : (h + 1) * 8, :] for g in gains)
-                    low = row[:8] < 4
-                    even = jnp.where(low, a, pltpu.roll(b, 4, 0))
-                    odd = jnp.where(low, pltpu.roll(a, 4, 0), b)
-                    yb = c * (CH // 4) + 2 * h
-                    for i, value in enumerate((even, odd)):
-                        bricks[(yb + i) * n_z + j, pl.ds(pl.multiple_of(8 * p, 8), 8), :] = value
-            return 0
-
-        lax.fori_loop(0, cx // 2, pair, 0)
-
-    to_scalar.wait()
-
-    def pack(dst, at, target):
+    half = cx // 2
+    base_near = half * (1 - lax.rem(me, 2))
+
+    def second_half(phase, take, base):
+        for c in range(n_c):
+            take(x2, 1, c)
+            flags = [mask(1, c, j) for j in range(n_z)]
+
+            def pair(p, _):
+                for j in range(n_z):
+                    gains = []
+                    for i in range(2):
+                        x = base + 2 * p + i
+                        before = x1[R + x, j, PAD + c * CH : PAD + (c + 1) * CH, :]
+                        here, new = following(x2, x, c, j, before, flags[j])
+                        spot = (slice(c * CH, (c + 1) * CH), slice(j * LANES, (j + 1) * LANES))
+                        second_v[(x,) + spot] = new
+                        gains.append(
+                            src_v[(0, x) + spot].astype(jnp.float32) * here
+                            + src_v[(1, x) + spot].astype(jnp.float32) * new
+                        )
+                    for h in range(CH // 8):
+                        a, b = (g[h * 8 : (h + 1) * 8, :] for g in gains)
+                        low = row[:8] < 4
+                        first = jnp.where(low, a, pltpu.roll(b, 4, 0))
+                        other = jnp.where(low, pltpu.roll(a, 4, 0), b)
+                        yb = c * (CH // 4) + 2 * h
+                        for i, value in enumerate((first, other)):
+                            at = (yb + i) * n_z + j
+                            bricks[phase, at, pl.ds(pl.multiple_of(8 * p, 8), 8), :] = value
+                return 0
+
+            lax.fori_loop(0, half // 2, pair, 0)
+
+    def pack(phase, k, target):
         for r in range(cap):
-            dst[at + r] = bricks[asked_s[target, 0, r]]
-
-    def give(k, target):
-        return pltpu.make_async_remote_copy(
-            src_ref=outgoing.at[pl.ds(k * cap, cap)],
-            dst_ref=incoming.at[pl.ds(me * cap, cap)],
+            outgoing[phase, k * cap + r] = bricks[phase, asked_s[target, 0, r]]
+
+    def landing(base):
+        rows = pl.ds(pl.multiple_of(base * 4, 16), half * 4)
+        return incoming.at[pl.ds(me * cap, cap), rows, :]
+
+    bases = (base_near, half - base_near)
+
+    def give(phase, k):
+        target = flipped(me, k, bits) if n == 2**bits else lax.rem(me + k, n)
+        pack(phase, k, target)
+        pltpu.make_async_remote_copy(
+            src_ref=outgoing.at[phase, pl.ds(k * cap, cap)],
+            dst_ref=landing(bases[phase]),
             send_sem=a2a_send,
             recv_sem=a2a_recv,
             device_id={"col": target},
             device_id_type=MESH,
-        )
-
-    def partner(k):
-        return flipped(me, k, bits) if n == 2**bits else lax.rem(me + k, n)
-
-    def start_give(i, _):
-        k = n - 1 - i
-        target = partner(k)
-        pack(outgoing, k * cap, target)
-        give(k, target).start()
-        return 0
-
-    lax.fori_loop(0, n - 1, start_give, 0)
+        ).start()
+
+    def give_group(phase, start, top, shift):
+        def one(i, _):
+            give(phase, top + (i // 2) * 4 + shift + i % 2)
+            return 0
+
+        lax.fori_loop(start, n // 4, one, 0)
+
+    def give_all(phase):
+        def one(i, _):
+            give(phase, i)
+            return 0
+
+        lax.fori_loop(1, n, one, 0)
+
+    grouped = n == 2**bits and n >= 8
+    second_half(0, take_near, bases[0])
+    to_scalar.wait()
+    if grouped:
+        give_group(0, 0, n // 2, 0)
+        give_group(0, 0, n // 2, 2)
+        give_group(0, 1, 0, 0)
+    else:
+        give_all(0)
+    second_half(1, take_other, bases[1])
+    if grouped:
+        give_group(1, 0, n // 2, 0)
+        give_group(1, 0, n // 2, 2)
+        give_group(0, 0, 0, 2)
+        give_group(1, 0, 0, 2)
+        give_group(1, 1, 0, 0)
+    else:
+        give_all(1)
 
     store_second = pltpu.make_async_copy(second_v, second_h, out_sem.at[n_z])
     store_second.start()
-    pack(outgoing, 0, me)
-    keep = pltpu.make_async_copy(
-        outgoing.at[pl.ds(0, cap)], incoming.at[pl.ds(me * cap, cap)], keep_sem
-    )
-    keep.start()
+    keeps = []
+    for phase in range(2):
+        pack(phase, 0, me)
+        keep = pltpu.make_async_copy(
+            outgoing.at[phase, pl.ds(0, cap)], landing(bases[phase]), keep_sem.at[phase]
+        )
+        keep.start()
+        keeps.append(keep)
 
     whole = pl.ds(cap, (n - 1) * cap)
     pltpu.make_async_copy(incoming.at[whole], incoming.at[whole], a2a_recv).wait()
@@ -343,8 +398,8 @@
     pltpu.make_async_copy(
         want_v.at[pl.ds(0, n - 1)], want_v.at[pl.ds(0, n - 1)], ask_send
     ).wait()
-    pltpu.make_async_copy(outgoing.at[whole], outgoing.at[whole], a2a_send).wait()
-    for copy in store_first + [store_second, keep]:
+    pltpu.make_async_copy(outgoing.at[:, whole], outgoing.at[:, whole], a2a_send).wait()
+    for copy in store_first + [store_second] + keeps:
         copy.wait()
 
 
@@ -423,8 +478,8 @@
             pltpu.VMEM((cx, ny, nz), f32),
             pltpu.VMEM((2, cx, ny, nz), jnp.bfloat16),
             pltpu.VMEM((cx, ny, nz), f32),
-            pltpu.VMEM((per, 32, LANES), f32),
-            pltpu.VMEM((n * cap, 32, LANES), f32),
+            pltpu.VMEM((2, per, 16, LANES), f32),
+            pltpu.VMEM((2, n * cap, 16, LANES), f32),
             pltpu.SMEM(active.shape, jnp.int32),
             pltpu.SMEM((per,), jnp.int32),
             pltpu.VMEM(((n + 7) // 8 * 8, LANES), jnp.int32),
@@ -439,7 +494,7 @@
             dma(()),
             dma(()),
             dma(()),
-            dma(()),
+            dma((2,)),
             dma((n_z + 1,)),
         ],
         compiler_params=pltpu.CompilerParams(

time: 58 us -> 55.1 us (0.950)
  the two profiles are of different devices: /device:TPU:1 before, /device:TPU:2 now
where the time goes in v4:
time: 55.1 us; the launch traced here: 55 us
  Pallas kernels  54.3 us (99%)
  between operations  0.64 us (1%)
    pallas_call x1, Pallas kernels, shards(): pl.pallas_call(functools.partial(kernel, n, cap), out_shape=(jax.ShapeDty...  50.2 us
    pallas_call x1, Pallas kernels, shards(): pl.pallas_call(finish, out_shape=(jax.ShapeDtypeStruct((cx, ny, nz), f32)...  4.13 us

profile of v4, /device:TPU:2, one launch (start us, length us, event | category | flops | bytes accessed | tf_op | source)
XLA Modules:
  0.0 55.0 jit_solution(14170350553727194633)
XLA Ops:
  0.6 50.2 %shard_map.94 = (f32[8,64,512]{2,1,0:T(8,128)}, f32[8,64,512]{2,1,0:T(8,128)}, f32[64,32,128]{2,1,0:T(8,128)}, s32[1,128]{1,0:T(1,128)}) custom-call(f32[8,64,512]{2,1,0:T(8,128)} %prev_h.1, f32[8,64,512]{2,1,0:T(8,128)} %now_h.1, f32[8,64,512]{2,1,0:T(8,128)} %vel_h.1, bf16[2,8,64,512]{3,2,1,0:T(8,128)(2,1)} %src_h.1, s32[2,64]{1,0:T(2,128)} %active_h.1, ...), custom_call_target="tpu_custom_call" | custom-call | tf_op jit(solution)/shard_map/pallas_call | solution.py:463
  50.9 4.1 %shard_map.95 = (f32[8,64,512]{2,1,0:T(8,128)}, f32[8,64,512]{2,1,0:T(8,128)}, f32[64,32,128]{2,1,0:T(8,128)}) custom-call(s32[1,128]{1,0:T(1,128)} %get-tuple-element.10.place_s, f32[8,64,512]{2,1,0:T(8,128)} %get-tuple-element.11.first_h, f32[8,64,512]{2,1,0:T(8,128)} %get-tuple-element.12.second_h, f32[64,32,128]{2,1,0:T(8,128)} %get-tuple-element.13.incoming_h, ...), custom_call_target="tpu_custom_call" | custom-call | tf_op jit(solution)/shard_map/pallas_call | solution.py:506

commit v5 on v4

--- a/solution.py
+++ b/solution.py
@@ -196,9 +196,9 @@
     lane = lax.broadcasted_iota(jnp.int32, (CH, LANES), 1)
     row = lax.broadcasted_iota(jnp.int32, (CH, LANES), 0)
 
-    def along_yz(buf):
+    def along_yz(buf, chunks):
         def plane(x, _):
-            for c in range(n_c):
+            for c in chunks:
                 tiles = [buf[R + x, j, PAD + c * CH : PAD + (c + 1) * CH, :] for j in range(n_z)]
                 for j in range(n_z):
                     total = (3.0 * COEF[0]) * tiles[j]
@@ -254,46 +254,15 @@
         def _():
             halo(buf, step, 1, c).wait_recv()
 
-    along_yz(x1)
-    load_prev.wait()
-    load_vel.wait()
-    for c in range(n_c):
-        take_halo(x1, 0, c)
-        flags = [mask(0, c, j) for j in range(n_z)]
-
-        def plane(x, _):
-            for j in range(n_z):
-                before = prev_v[x, c * CH : (c + 1) * CH, j * LANES : (j + 1) * LANES]
-                _, new = following(x1, x, c, j, before, flags[j])
-                x2[R + x, j, PAD + c * CH : PAD + (c + 1) * CH, :] = new
-            return 0
-
-        lax.fori_loop(0, cx, plane, 0)
-        send_halo(x2, 1, c)
-
-    store_first = [
-        pltpu.make_async_copy(
-            x2.at[own, j, body, :], first_h.at[:, :, pl.ds(j * LANES, LANES)], out_sem.at[j]
-        )
-        for j in range(n_z)
-    ]
-    for copy in store_first:
-        copy.start()
-
-    along_yz(x2)
-
-    pltpu.make_async_copy(
-        asked_v.at[pl.ds(0, n - 1)], asked_v.at[pl.ds(0, n - 1)], ask_recv
-    ).wait()
-    to_scalar = pltpu.make_async_copy(asked_v, asked_s, ask_copy)
-    to_scalar.start()
-
-    load_src.wait()
+    along_yz(x1, range(n_c))
     half = cx // 2
     base_near = half * (1 - lax.rem(me, 2))
 
-    def second_half(phase, take, base):
-        for c in range(n_c):
+    bases = (base_near, half - base_near)
+
+    def second_half(phase, take, chunks):
+        base = bases[phase]
+        for c in chunks:
             take(x2, 1, c)
             flags = [mask(1, c, j) for j in range(n_z)]
 
@@ -323,6 +292,35 @@
 
             lax.fori_loop(0, half // 2, pair, 0)
 
+    pltpu.make_async_copy(
+        asked_v.at[pl.ds(0, n - 1)], asked_v.at[pl.ds(0, n - 1)], ask_recv
+    ).wait()
+    to_scalar = pltpu.make_async_copy(asked_v, asked_s, ask_copy)
+    to_scalar.start()
+    load_prev.wait()
+    load_vel.wait()
+    for c in range(n_c):
+        take_halo(x1, 0, c)
+        flags = [mask(0, c, j) for j in range(n_z)]
+
+        def plane(x, _):
+            for j in range(n_z):
+                before = prev_v[x, c * CH : (c + 1) * CH, j * LANES : (j + 1) * LANES]
+                _, new = following(x1, x, c, j, before, flags[j])
+                x2[R + x, j, PAD + c * CH : PAD + (c + 1) * CH, :] = new
+            return 0
+
+        lax.fori_loop(0, cx, plane, 0)
+        send_halo(x2, 1, c)
+        if c > 0:
+            along_yz(x2, [c - 1])
+        if c == 1:
+            load_src.wait()
+        if c > 1:
+            second_half(0, take_near, [c - 2])
+    along_yz(x2, [n_c - 1])
+    second_half(0, take_near, [n_c - 2, n_c - 1])
+
     def pack(phase, k, target):
         for r in range(cap):
             outgoing[phase, k * cap + r] = bricks[phase, asked_s[target, 0, r]]
@@ -330,8 +328,6 @@
     def landing(base):
         rows = pl.ds(pl.multiple_of(base * 4, 16), half * 4)
         return incoming.at[pl.ds(me * cap, cap), rows, :]
-
-    bases = (base_near, half - base_near)
 
     def give(phase, k):
         target = flipped(me, k, bits) if n == 2**bits else lax.rem(me + k, n)
@@ -360,7 +356,6 @@
         lax.fori_loop(1, n, one, 0)
 
     grouped = n == 2**bits and n >= 8
-    second_half(0, take_near, bases[0])
     to_scalar.wait()
     if grouped:
         give_group(0, 0, n // 2, 0)
@@ -368,7 +363,15 @@
         give_group(0, 1, 0, 0)
     else:
         give_all(0)
-    second_half(1, take_other, bases[1])
+    store_first = [
+        pltpu.make_async_copy(
+            x2.at[own, j, body, :], first_h.at[:, :, pl.ds(j * LANES, LANES)], out_sem.at[j]
+        )
+        for j in range(n_z)
+    ]
+    for copy in store_first:
+        copy.start()
+    second_half(1, take_other, range(n_c))
     if grouped:
         give_group(1, 0, n // 2, 0)
         give_group(1, 0, n // 2, 2)

time: 55.1 us -> 54 us (0.980)
  the two profiles are of different devices: /device:TPU:2 before, /device:TPU:3 now
where the time goes in v5:
time: 54 us; the launch traced here: 53.8 us
  Pallas kernels  53.2 us (99%)
  between operations  0.64 us (1%)
    pallas_call x1, Pallas kernels, shards(): pl.pallas_call(functools.partial(kernel, n, cap), out_shape=(jax.ShapeDty...  49.1 us
    pallas_call x1, Pallas kernels, shards(): pl.pallas_call(finish, out_shape=(jax.ShapeDtypeStruct((cx, ny, nz), f32)...  4.13 us

profile of v5, /device:TPU:3, one launch (start us, length us, event | category | flops | bytes accessed | tf_op | source)
XLA Modules:
  0.0 53.8 jit_solution(18326710052528069323)
XLA Ops:
  0.6 49.1 %shard_map.94 = (f32[8,64,512]{2,1,0:T(8,128)}, f32[8,64,512]{2,1,0:T(8,128)}, f32[64,32,128]{2,1,0:T(8,128)}, s32[1,128]{1,0:T(1,128)}) custom-call(f32[8,64,512]{2,1,0:T(8,128)} %prev_h.1, f32[8,64,512]{2,1,0:T(8,128)} %now_h.1, f32[8,64,512]{2,1,0:T(8,128)} %vel_h.1, bf16[2,8,64,512]{3,2,1,0:T(8,128)(2,1)} %src_h.1, s32[2,64]{1,0:T(2,128)} %active_h.1, ...), custom_call_target="tpu_custom_call" | custom-call | tf_op jit(solution)/shard_map/pallas_call | solution.py:466
  49.7 4.1 %shard_map.95 = (f32[8,64,512]{2,1,0:T(8,128)}, f32[8,64,512]{2,1,0:T(8,128)}, f32[64,32,128]{2,1,0:T(8,128)}) custom-call(s32[1,128]{1,0:T(1,128)} %get-tuple-element.10.place_s, f32[8,64,512]{2,1,0:T(8,128)} %get-tuple-element.11.first_h, f32[8,64,512]{2,1,0:T(8,128)} %get-tuple-element.12.second_h, f32[64,32,128]{2,1,0:T(8,128)} %get-tuple-element.13.incoming_h, ...), custom_call_target="tpu_custom_call" | custom-call | tf_op jit(solution)/shard_map/pallas_call | solution.py:509
